TPU v7x, 128 devices: a whole 4x4x4 slice. The times are simulated.
128 devices in a mesh: grp: 4 (over x), smp: 32 (over y, z, core).
Axes of the slice: x: 4, y: 4, z: 4, core: 2. Of those that a mesh axis runs over, the one named last changes fastest.
Arguments:
- hidden: bfloat16 [4, 128, 4, 3584], P('grp', 'smp'), may hold values from -3 to 3
- query: bfloat16 [4, 128, 4, 64, 576], P('grp', 'smp'), may hold values from -40 to 40
- prefill_cache: bfloat16 [4, 8, 2048, 576], P('grp', None, 'smp'), may hold values from -4.5 to 4.5
- suffix_cache: bfloat16 [4, 128, 128, 576], P('grp', 'smp'), may hold values from -4 to 4
- suffix_len: int32 [4, 128], P('grp', 'smp'), may hold values from 1 to 128, 8192 in all within a row
- new_latent: bfloat16 [4, 128, 4, 576], P('grp', 'smp'), may hold values from -4 to 4
- w_uv: bfloat16 [64, 512, 128], P('smp'), may hold values from -0.25 to 0.25
- w_out: bfloat16 [64, 128, 3584], P('smp'), may hold values from -0.25 to 0.25
- ffn_gain: bfloat16 [3584], replicated, may hold values from 0.099609375 to 1.8984375
- expert_ids: int32 [4, 128, 4, 8], P('grp', 'smp'), may hold values from 0 to 127, all different within a row; in each aligned block of 16 rows (0 to 15, 16 to 31, ..., all dimensions but the last counted through in order) at most 2 rows name the same one
- route_weights: float32 [4, 128, 4, 8], P('grp', 'smp'), may hold values from 0.05 to 0.5
- w_gate: bfloat16 [128, 3584, 1024], P(('grp', 'smp')), may hold values from -0.09375 to 0.09375
- w_up: bfloat16 [128, 3584, 1024], P(('grp', 'smp')), may hold values from -0.09375 to 0.09375
- w_down: bfloat16 [128, 1024, 3584], P(('grp', 'smp')), may hold values from -0.1875 to 0.1875
Outputs:
- layer_out: bfloat16 [4, 128, 4, 3584], P('grp', 'smp')
Inputs may be any that keep to these rules, and one draw needn't show every extreme that they name: `expert_ids`: the rows of one device name one expert at most 2 times; every expert is named by some row.
All inputs are finite; a program needn't handle non-finite values. No bound on the sum of `suffix_len` on one device may be relied on, other than what follows from the above.
Results may differ from a plain program's by a relative error of at most 0.024.
Values may be sent and summed in bfloat16 or wider, within the bound.
No kernel may reach another device: no remote copies, remote signals or barrier semaphores. Data moves between devices by JAX's collectives and lax.ppermute only.
A program may use at most 128 MiB of HBM per device.

v0:
```python
import jax
import jax.numpy as jnp
from jax import lax
from jax.sharding import PartitionSpec as P

D = 3584
HEADS = 64
LAT = 512
ROPE = 64
NOPE = 128
TOP = 8
GROUP = 16
STEPS = 4
SUF = 128


def attend(queries, prefix, own_cache, own_len, fresh):
    samples = queries.shape[0]
    key_width = queries.shape[-1]
    query_rows = queries.reshape(samples, STEPS * HEADS, key_width)
    softmax_scale = (NOPE + ROPE) ** (-0.5)
    score_prefix = (
        jnp.einsum("srl,kl->srk", query_rows, prefix, preferred_element_type=jnp.float32)
        * softmax_scale
    )
    score_own = (
        jnp.einsum("srl,skl->srk", query_rows, own_cache, preferred_element_type=jnp.float32)
        * softmax_scale
    )
    score_fresh = (
        jnp.einsum("srl,stl->srt", query_rows, fresh, preferred_element_type=jnp.float32)
        * softmax_scale
    )
    own_mask = jnp.arange(SUF, dtype=jnp.int32)[None, None, :] < own_len[:, None, None]
    row_step = jnp.arange(STEPS * HEADS, dtype=jnp.int32) // HEADS
    fresh_mask = (jnp.arange(STEPS, dtype=jnp.int32)[None, :] <= row_step[:, None])[None]
    score_own = jnp.where(own_mask, score_own, -jnp.inf)
    score_fresh = jnp.where(fresh_mask, score_fresh, -jnp.inf)
    rowmax = jnp.maximum(
        jnp.max(score_prefix, -1), jnp.maximum(jnp.max(score_own, -1), jnp.max(score_fresh, -1))
    )[..., None]
    expo_prefix = jnp.exp(score_prefix - rowmax)
    expo_own = jnp.exp(score_own - rowmax)
    expo_fresh = jnp.exp(score_fresh - rowmax)
    denominator = jnp.sum(expo_prefix, -1) + jnp.sum(expo_own, -1) + jnp.sum(expo_fresh, -1)
    numerator = jnp.einsum(
        "srk,kl->srl",
        expo_prefix.astype(jnp.bfloat16),
        prefix[:, :LAT],
        preferred_element_type=jnp.float32,
    )
    numerator = numerator + jnp.einsum(
        "srk,skl->srl",
        expo_own.astype(jnp.bfloat16),
        own_cache[:, :, :LAT],
        preferred_element_type=jnp.float32,
    )
    numerator = numerator + jnp.einsum(
        "srt,stl->srl",
        expo_fresh.astype(jnp.bfloat16),
        fresh[:, :, :LAT],
        preferred_element_type=jnp.float32,
    )
    context = (numerator / denominator[..., None]).astype(jnp.bfloat16)
    return context.reshape(samples, STEPS, HEADS, LAT)


def on_device(
    hidden,
    query,
    prefill_cache,
    suffix_cache,
    suffix_len,
    new_latent,
    w_uv,
    w_out,
    ffn_gain,
    expert_ids,
    route_weights,
    w_gate,
    w_up,
    w_down,
):
    samp_here = query.shape[1]
    tok_here = samp_here * query.shape[2]
    slab = prefill_cache[0]
    prompt_here = lax.axis_index("smp") * samp_here // GROUP
    gathered = lax.all_gather(slab, "smp", axis=1, tiled=True)
    prefix = lax.dynamic_index_in_dim(gathered, prompt_here, 0, keepdims=False)
    context = attend(query[0], prefix, suffix_cache[0], suffix_len[0], new_latent[0])
    by_heads = lax.all_to_all(context, "smp", split_axis=2, concat_axis=0, tiled=True)
    flat_context = by_heads.reshape(-1, by_heads.shape[2], by_heads.shape[3])
    head_value = jnp.einsum(
        "rhl,hlv->rhv", flat_context, w_uv, preferred_element_type=jnp.float32
    ).astype(jnp.bfloat16)
    attention = lax.psum_scatter(
        jnp.einsum("rhv,hvd->rd", head_value, w_out, preferred_element_type=jnp.float32).astype(
            jnp.bfloat16
        ),
        "smp",
        scatter_dimension=0,
        tiled=True,
    ).astype(jnp.float32)
    residual = hidden.reshape(tok_here, D).astype(jnp.float32) + attention
    mean_square = jnp.mean(residual * residual, axis=-1, keepdims=True)
    normalized = (residual * lax.rsqrt(mean_square + 1e-06) * ffn_gain.astype(jnp.float32)).astype(
        jnp.bfloat16
    )
    experts_all = lax.axis_size("grp") * lax.axis_size("smp")
    capacity = max(2, 2 * tok_here * TOP // experts_all)
    route_flat = expert_ids.reshape(-1)
    onehot = (route_flat[:, None] == jnp.arange(experts_all, dtype=jnp.int32)[None, :]).astype(
        jnp.int32
    )
    earlier = jnp.cumsum(onehot, axis=0) - onehot
    slot_index = jnp.sum(onehot * earlier, axis=1)
    destination = route_flat * capacity + slot_index
    sent_rows = jnp.repeat(normalized, TOP, axis=0)
    outgoing_rows = (
        jnp.zeros((experts_all * capacity, D), jnp.bfloat16).at[destination].set(sent_rows)
    )
    grouped = outgoing_rows.reshape(experts_all, capacity, D)
    arrived = lax.all_to_all(grouped, ("grp", "smp"), split_axis=0, concat_axis=0, tiled=True)
    flat_rows = arrived.reshape(-1, D)
    gate_out = jnp.dot(flat_rows, w_gate[0], preferred_element_type=jnp.float32)
    up_out = jnp.dot(flat_rows, w_up[0], preferred_element_type=jnp.float32)
    middle = (jax.nn.silu(gate_out) * up_out).astype(jnp.bfloat16)
    result = jnp.dot(middle, w_down[0], preferred_element_type=jnp.float32).astype(jnp.bfloat16)
    answered = result.reshape(arrived.shape)
    returned = lax.all_to_all(answered, ("grp", "smp"), split_axis=0, concat_axis=0, tiled=True)
    gathered_back = returned.reshape(experts_all * capacity, D)[destination]
    expert_rows = gathered_back.reshape(tok_here, TOP, D).astype(jnp.float32)
    weights_here = route_weights.reshape(tok_here, TOP, 1)
    mixture = jnp.sum(expert_rows * weights_here, axis=1)
    layer_out = (residual + mixture).astype(jnp.bfloat16)
    return layer_out.reshape(hidden.shape)


def solution(mesh):
    placed = (
        P("grp", "smp", None, None),
        P("grp", "smp", None, None, None),
        P("grp", None, "smp", None),
        P("grp", "smp", None, None),
        P("grp", "smp"),
        P("grp", "smp", None, None),
        P("smp", None, None),
        P("smp", None, None),
        P(),
        P("grp", "smp", None, None),
        P("grp", "smp", None, None),
        P(("grp", "smp"), None, None),
        P(("grp", "smp"), None, None),
        P(("grp", "smp"), None, None),
    )
    return jax.shard_map(
        on_device,
        mesh=mesh,
        in_specs=placed,
        out_specs=P("grp", "smp", None, None),
        check_vma=False,
    )
```

profile of v0, /device:TPU:1, one launch (start us, length us, event | category | flops | bytes accessed | tf_op | source)
XLA Modules:
  0.0 337.6 jit_solution(10815700510745260597)
XLA Ops:
  6.5 0.0 copy-start
  6.5 0.0 all-gather.3.cloned.1.call-start
  6.5 0.7 all-gather.3.cloned.1.call-update
  7.3 0.0 reduce-scatter.2.cloned.1.call-start
  7.3 2.1 copy.47
  9.5 0.7 iota_compare_fusion.2
  10.2 1.8 fusion.55
  12.0 2.4 fusion.54
  14.4 81.4 %all-gather.3.cloned.1.call-done = bf16[1,8,2048,576]{3,2,1,0:T(8,128)(2,1)} async-done(((bf16[1,8,64,576]{3,2,1,0:T(8,128)(2,1)}), bf16[1,8,2048,576]{3,2,1,0:T(8,128)(2,1)}) %all-gather.3.cloned.1.call-update) | async-done | bytes 18874384 | tf_op jit(solution)/shard_map/all_gather | solution.py:88
  95.8 3.5 %constant_dynamic-slice_fusion = bf16[1,1,2048,576]{3,2,1,0:T(8,128)(2,1)} fusion(bf16[1,8,2048,576]{3,2,1,0:T(8,128)(2,1)} %all-gather.3.cloned.1.call-done, s32[]{:T(128)S(6)} %select_n.38), kind=kLoop, calls=%fused_computation.71 | loop fusion | bytes 4718596 | tf_op jit(solution)/shard_map/jit(dynamic_index_in_dim)/dynamic_slice | solution.py:89
  99.3 4.5 %copy.45 = bf16[1,1,2048,576]{2,3,1,0:T(8,128)(2,1)} copy(bf16[1,1,2048,576]{3,2,1,0:T(8,128)(2,1)} %constant_dynamic-slice_fusion) | data formatting | bytes 4718592 | tf_op jit(solution)/shard_map/jit(dynamic_index_in_dim)/dynamic_slice | solution.py:89
  103.7 5.3 %bitcast_reduce_fusion = (f32[4,256]{1,0:T(4,128)S(1)}, f32[2048,4,256]{2,0,1:T(8,128)S(1)}) fusion(bf16[4,256,576]{2,1,0:T(8,128)(2,1)S(1)} %bitcast.85, bf16[1,1,2048,576]{3,2,1,0:T(8,128)(2,1)} %constant_dynamic-slice_fusion), kind=kOutput, calls=%fused_computation.3 | convolution fusion | flops 2420112384 | bytes 11931648 | tf_op jit(solution)/shard_map/srl,kl->srk/dot_general | solution.py:23
  109.0 1.4 fusion.7
  110.4 0.3 copy-done.4
  110.7 2.4 fusion.12
  113.1 0.0 copy-start.10
  113.1 0.1 fusion.39
  113.2 0.5 fusion.36
  113.7 0.1 copy-done.10
  113.8 0.6 divide_convert_fusion
  114.4 0.8 copy.54
  115.2 0.0 copy-start.7
  115.2 22.2 %all_to_all.25 = bf16[4,4,64,512]{3,1,0,2:T(4,128)(2,1)S(1)} all-to-all(bf16[4,4,64,512]{3,1,0,2:T(4,128)(2,1)S(1)} %copy.54), channel_id=1, replica_groups=mesh['grp'=4,'smp'=32] {'smp'}, dimensions={2} | all-to-all | bytes 2097152 | tf_op jit(solution)/shard_map/all_to_all | solution.py:91
  137.4 1.7 copy.56
  139.2 3.0 bitcast_convert_fusion
  142.2 0.0 reduce-scatter.2.cloned.1.call-update
  142.2 0.7 copy-done.9
  142.8 0.1 eq.15
  142.9 0.1 mul.89
  143.1 0.1 fusion.44
  143.1 0.2 reduce_window_sum.11
  143.3 0.2 select_reduce_fusion
  143.5 76.0 %reduce-scatter.2.cloned.1.call-done = bf16[16,3584]{1,0:T(8,128)(2,1)} async-done(((bf16[512,3584]{1,0:T(8,128)(2,1)}), bf16[16,3584]{1,0:T(8,128)(2,1)}) %reduce-scatter.2.cloned.1.call-update) | async-done | bytes 114704 | tf_op jit(solution)/shard_map/reduce_scatter | solution.py:96
  219.5 1.0 multiply_reduce_fusion
  220.6 1.0 multiply_convert_fusion
  221.6 3.3 scatter_custom_fusion
  224.9 3.9 %reshape.147 = bf16[128,2,3584]{2,1,0:T(2,128)(2,1)S(1)} reshape(bf16[256,3584]{1,0:T(8,128)(2,1)} %scatter_custom_fusion) | data formatting | bytes 3670016 | tf_op jit(solution)/shard_map/reshape | solution.py:122
  228.8 36.7 %all_to_all.26 = bf16[128,2,3584]{2,1,0:T(2,128)(2,1)} all-to-all(bf16[128,2,3584]{2,1,0:T(2,128)(2,1)S(1)} %reshape.147), channel_id=1, replica_groups=mesh['grp'=4,'smp'=32] {'grp','smp'}, dimensions={0} | all-to-all | bytes 3670016 | tf_op jit(solution)/shard_map/all_to_all | solution.py:123
  265.5 4.1 %reshape.148 = bf16[256,3584]{1,0:T(8,128)(2,1)S(1)} reshape(bf16[128,2,3584]{2,1,0:T(2,128)(2,1)} %all_to_all.26) | data formatting | bytes 3670016 | tf_op jit(solution)/shard_map/reshape | solution.py:124
  269.6 6.1 %fusion.5 = f32[256,1024]{1,0:T(8,128)} fusion(bf16[256,3584]{1,0:T(8,128)(2,1)S(1)} %reshape.148, bf16[1,3584,1024]{2,1,0:T(8,128)(2,1)} %param.25), kind=kOutput, calls=%fused_computation.9 | convolution fusion | flops 1879048192 | bytes 10223616 | tf_op jit(solution)/shard_map/dot_general | solution.py:125
  275.7 10.8 %fusion.9 = bf16[256,3584]{1,0:T(8,128)(2,1)} fusion(bf16[1,1024,3584]{2,1,0:T(8,128)(2,1)} %param.27, bf16[256,3584]{1,0:T(8,128)(2,1)S(1)} %reshape.148, bf16[1,3584,1024]{2,1,0:T(8,128)(2,1)} %param.26, f32[256,1024]{1,0:T(8,128)} %fusion.5), kind=kOutput, calls=%fused_computation.14 | convolution fusion | flops 3760586752 | bytes 19398656 | tf_op jit(solution)/shard_map/dot_general | solution.py:128
  286.5 4.7 %reshape.149 = bf16[128,2,3584]{2,1,0:T(2,128)(2,1)} reshape(bf16[256,3584]{1,0:T(8,128)(2,1)} %fusion.9) | data formatting | bytes 3670016 | tf_op jit(solution)/shard_map/reshape | solution.py:129
  291.2 4.6 %all-to-all-start.2 = ((bf16[128,2,3584]{2,1,0:T(2,128)(2,1)}), bf16[128,2,3584]{2,1,0:T(2,128)(2,1)S(1)}, u32[]{:S(2)}, u32[]{:S(2)}) async-start(bf16[128,2,3584]{2,1,0:T(2,128)(2,1)} %reshape.149), calls=%async_computation.3 | async-start | bytes 3670016 | tf_op jit(solution)/shard_map/all_to_all | solution.py:130
  295.9 27.8 %all-to-all-done.2 = bf16[128,2,3584]{2,1,0:T(2,128)(2,1)S(1)} async-done(((bf16[128,2,3584]{2,1,0:T(2,128)(2,1)}), bf16[128,2,3584]{2,1,0:T(2,128)(2,1)S(1)}, u32[]{:S(2)}, u32[]{:S(2)}) %all-to-all-start.2) | async-done | bytes 1835040 | tf_op jit(solution)/shard_map/all_to_all | solution.py:130
  323.7 1.7 reshape.150
  325.4 3.9 %gather_fusion = bf16[128,3584]{1,0:T(8,128)(2,1)S(1)} fusion(bf16[256,3584]{1,0:T(8,128)(2,1)} %reshape.150, s32[1024]{0:T(1024)S(1)} %pad_clamp_fusion), kind=kCustom, calls=%fused_computation | custom fusion | bytes 1835520 | tf_op jit(solution)/shard_map/gather | solution.py:131
  329.3 0.7 fusion.18
  330.0 0.7 reshape.151
  (32 shorter events, 0.2 us)
Async XLA Ops:
  6.5 132.6 %copy-start = (bf16[2,128,3584]{2,1,0:T(8,128)(2,1)S(1)}, bf16[2,128,3584]{2,1,0:T(8,128)(2,1)}, u32[]{:S(2)}) copy-start(bf16[2,128,3584]{2,1,0:T(8,128)(2,1)} %param.21) | copy-start | bytes 5505028
  6.5 5.5 %copy-start.2 = (bf16[1,4,4,64,576]{4,3,2,1,0:T(8,128)(2,1)S(1)}, bf16[1,4,4,64,576]{4,3,2,1,0:T(8,128)(2,1)}, u32[]{:S(2)}) copy-start(bf16[1,4,4,64,576]{4,3,2,1,0:T(8,128)(2,1)} %param.15) | copy-start | bytes 3538948
  6.5 89.3 %all-gather.3.cloned.1.call-start = ((), (), s32[]{:S(2)}) async-start(), calls=%async_computation.5 | async-start | bytes 21626880 | tf_op jit(solution)/shard_map/all_gather | solution.py:88
  7.3 212.2 %reduce-scatter.2.cloned.1.call-start = ((), (), s32[]{:S(2)}) async-start(), calls=%async_computation.4 | async-start | bytes 3784704 | tf_op jit(solution)/shard_map/reduce_scatter | solution.py:96
  109.0 1.7 copy-start.4
  110.7 2.4 copy-start.3
  110.7 2.5 copy-start.5
  113.1 0.7 copy-start.10
  115.2 24.0 %copy-start.7 = (bf16[2,512,128]{2,1,0:T(8,128)(2,1)S(1)}, bf16[2,512,128]{2,1,0:T(8,128)(2,1)}, u32[]{:S(2)}) copy-start(bf16[2,512,128]{2,1,0:T(8,128)(2,1)} %param.20) | copy-start | bytes 786436
  142.1 0.7 copy-start.9
  142.1 0.9 copy-start.12
  142.1 1.2 copy-start.8
  291.2 32.5 %all-to-all-start.2 = ((bf16[128,2,3584]{2,1,0:T(2,128)(2,1)}), bf16[128,2,3584]{2,1,0:T(2,128)(2,1)S(1)}, u32[]{:S(2)}, u32[]{:S(2)}) async-start(bf16[128,2,3584]{2,1,0:T(2,128)(2,1)} %reshape.149), calls=%async_computation.3 | async-start | bytes 3670016 | tf_op jit(solution)/shard_map/all_to_all | solution.py:130
  325.4 3.9 %copy-start.11 = (f32[1,4,4,8]{3,2,1,0:T(4,128)S(1)}, f32[1,4,4,8]{3,2,1,0:T(4,128)}, u32[]{:S(2)}) copy-start(f32[1,4,4,8]{3,2,1,0:T(4,128)} %param.24) | copy-start | bytes 1540
  325.4 4.6 %copy-start.6 = (bf16[16,3584]{1,0:T(8,128)(2,1)S(1)}, bf16[16,3584]{1,0:T(8,128)(2,1)}, u32[]{:S(2)}) copy-start(bf16[16,3584]{1,0:T(8,128)(2,1)} %reduce-scatter.2.cloned.1.call-done) | copy-start | bytes 344068
  325.4 5.3 %copy-start.1 = (bf16[2,128,3584]{2,1,0:T(8,128)(2,1)S(1)}, bf16[2,128,3584]{2,1,0:T(8,128)(2,1)}, u32[]{:S(2)}) copy-start(bf16[2,128,3584]{2,1,0:T(8,128)(2,1)} %param.21) | copy-start | bytes 5505028
Sparse Core Ops, SparseCore 0:
  9.7 86.0 all-gather.2
  142.3 77.1 reduce-scatter.1
where the time goes:
time: 338 us
  waiting for transfers between devices  186 us (55%)
  blocking collectives  58.9 us (17%)
  local copies, waits for them, and re-layouts  36.2 us (11%)
  matrix products  32.8 us (10%)
  between operations  13.7 us (4%)
  other arithmetic  5.46 us (2%)
  starting transfers between devices  4.64 us (1%)
    all_gather x1, waiting for transfers between devices, on_device(): gathered = lax.all_gather(slab, 'smp', axis=1, tiled=True)  81.4 us
    reduce_scatter x1, waiting for transfers between devices, on_device(): lax.psum_scatter(jnp.einsum('rhv,hvd->rd', head_value, w_out, preferred_e...  76 us
    all_to_all x1, blocking collectives, on_device(): lax.all_to_all(grouped, ('grp', 'smp'), split_axis=0, concat_axis=0, tile...  36.7 us
    all_to_all x1, waiting for transfers between devices, on_device(): lax.all_to_all(answered, ('grp', 'smp'), split_axis=0, concat_axis=0, til...  27.8 us
    all_to_all x1, blocking collectives, on_device(): lax.all_to_all(context, 'smp', split_axis=2, concat_axis=0, tiled=True)  22.2 us
    dot_general x1, matrix products, on_device(): jnp.dot(middle, w_down[0], preferred_element_type=jnp.float32)  10.8 us
    dynamic_slice x2, local copies, waits for them, and re-layouts, on_device(): prefix = lax.dynamic_index_in_dim(gathered, prompt_here, 0, keepdims=False)  7.94 us
  transfers between devices with their start and end apart: 3, of which 3 were waited for; matrix products, arithmetic and copies ran while one was open for 2% of the time, Pallas kernels for 0%

commit v1 on v0

v1 whole, which is shorter than its diff:
```python
import jax
import jax.numpy as jnp
from jax import lax
from jax.experimental import pallas as pl
from jax.experimental.pallas import tpu as pltpu
from jax.sharding import PartitionSpec as P

D = 3584
HEADS = 64
LAT = 512
ROPE = 64
NOPE = 128
FF = 1024
TOP = 8
STEPS = 4
SUF = 128
TOK = 16
EXPERTS = 128
QTR = 4
WIDE = D // QTR
SCALE = (NOPE + ROPE) ** (-0.5)
F32 = jnp.float32
BF16 = jnp.bfloat16
VMEM_LIMIT = 56 * 1024 * 1024


def dot(a, b):
    return jnp.dot(a, b, preferred_element_type=F32)


def dot_t(a, b):
    return lax.dot_general(a, b, (((1,), (1,)), ((), ())), preferred_element_type=F32)


def iota(shape, dim):
    return lax.broadcasted_iota(jnp.int32, shape, dim)


def params():
    return pltpu.CompilerParams(vmem_limit_bytes=VMEM_LIMIT)


def attend_body(len_ref, q_ref, ka_ref, kb_ref, own_ref, fresh_ref, out_ref, held):
    s = pl.program_id(0)
    q = q_ref[0]
    rows = STEPS * HEADS
    keys = [ka_ref[...], kb_ref[...], own_ref[0], fresh_ref[0]]
    scores = [dot_t(q, k) for k in keys]
    scores[2] = jnp.where(iota((rows, SUF), 1) < len_ref[0, s], scores[2], -jnp.inf)
    step = iota((rows, STEPS), 0) // HEADS
    scores[3] = jnp.where(iota((rows, STEPS), 1) <= step, scores[3], -jnp.inf)
    top = jnp.max(scores[0], -1, keepdims=True)
    for sc in scores[1:]:
        top = jnp.maximum(top, jnp.max(sc, -1, keepdims=True))
    total = jnp.zeros((rows, 1), F32)
    acc = jnp.zeros((rows, LAT), F32)
    for sc, k in zip(scores, keys):
        p = jnp.exp((sc - top) * SCALE)
        total = total + jnp.sum(p, -1, keepdims=True)
        acc = acc + dot(p.astype(BF16), k[:, :LAT])
    ctx = (acc / total).astype(BF16)
    for t in range(STEPS):
        held[s * STEPS + t] = ctx[t * HEADS : (t + 1) * HEADS]

    @pl.when(s == pl.num_programs(0) - 1)
    def _():
        n = TOK * 16
        perm = (iota((n, n), 1) == (iota((n, n), 0) % TOK) * 16 + iota((n, n), 0) // TOK).astype(BF16)
        for b in range(HEADS // 16):
            part = held[:, b * 16 : (b + 1) * 16, :].reshape(n, LAT)
            out_ref[b * 16 : (b + 1) * 16] = dot(perm, part).astype(BF16).reshape(16, TOK, LAT)


def attend(lens, q, ka, kb, own, fresh):
    samples, rows, width = q.shape
    half = ka.shape[0]
    return pl.pallas_call(
        attend_body,
        grid=(samples,),
        in_specs=[
            pl.BlockSpec(memory_space=pltpu.SMEM),
            pl.BlockSpec((1, rows, width), lambda i: (i, 0, 0)),
            pl.BlockSpec((half, width), lambda i: (0, 0)),
            pl.BlockSpec((half, width), lambda i: (0, 0)),
            pl.BlockSpec((1, SUF, width), lambda i: (i, 0, 0)),
            pl.BlockSpec((1, STEPS, width), lambda i: (i, 0, 0)),
        ],
        out_specs=pl.BlockSpec((HEADS, TOK, LAT), lambda i: (0, 0, 0)),
        out_shape=jax.ShapeDtypeStruct((HEADS, TOK, LAT), BF16),
        scratch_shapes=[pltpu.VMEM((TOK, HEADS, LAT), BF16)],
        compiler_params=params(),
        cost_estimate=pl.CostEstimate(
            flops=2 * samples * rows * (2 * half + SUF) * (width + LAT),
            bytes_accessed=8 * 1024 * 1024,
            transcendentals=samples * rows * (2 * half + SUF),
        ),
        name="attend",
    )(lens, q, ka, kb, own, fresh)


def project_body(core_ref, x_ref, uva_ref, uvb_ref, oa_ref, ob_ref, out_ref, hv):
    chips, _, tok, _ = x_ref.shape
    rows = chips * tok

    @pl.when(pl.program_id(0) == 0)
    def _():
        core = core_ref[0]
        for side, uv in enumerate((uva_ref, uvb_ref)):
            first = 2 * core if side == 0 else 2 * (1 - core)
            for h in range(2):
                xh = x_ref[:, pl.ds(first + h, 1)].reshape(rows, LAT)
                hv[side, :, h * NOPE : (h + 1) * NOPE] = dot(xh, uv[h]).astype(BF16)

    width = out_ref.shape[-1]
    y = dot(hv[0], oa_ref[...].reshape(2 * NOPE, width)) + dot(hv[1], ob_ref[...].reshape(2 * NOPE, width))
    out_ref[...] = y.astype(BF16).reshape(chips, tok, width)


def project(core, x, uva, uvb, oa, ob):
    chips, _, tok, _ = x.shape
    whole = lambda shape: pl.BlockSpec(shape, lambda i: (0,) * len(shape))
    cols = lambda shape: pl.BlockSpec(shape, lambda i: (0, 0, i))
    return pl.pallas_call(
        project_body,
        grid=(QTR,),
        in_specs=[
            pl.BlockSpec(memory_space=pltpu.SMEM),
            whole(x.shape),
            whole(uva.shape),
            whole(uvb.shape),
            cols((2, NOPE, WIDE)),
            cols((2, NOPE, WIDE)),
        ],
        out_specs=cols((chips, tok, WIDE)),
        out_shape=jax.ShapeDtypeStruct((chips, tok, D), BF16),
        scratch_shapes=[pltpu.VMEM((2, chips * tok, 2 * NOPE), BF16)],
        compiler_params=params(),
        cost_estimate=pl.CostEstimate(flops=1100000000, bytes_accessed=7 * 1024 * 1024, transcendentals=0),
        name="project",
    )(core, x, uva, uvb, oa, ob)


def route_body(ids_ref, w_ref, send_ref, mix_ref):
    lines = EXPERTS * 2 * QTR
    ids = ids_ref[...]
    w = w_ref[...]
    lane = iota((TOK, EXPERTS), 1)
    named = jnp.zeros((TOK, EXPERTS), F32)
    weight = jnp.zeros((TOK, EXPERTS), F32)
    for k in range(TOP):
        hit = ids[:, k : k + 1] == lane
        named = named + jnp.where(hit, 1.0, 0.0)
        weight = weight + jnp.where(hit, w[:, k : k + 1], 0.0)
    below = (iota((TOK, TOK), 1) < iota((TOK, TOK), 0)).astype(BF16)
    earlier = dot(below, named.astype(BF16))
    spread = (iota((EXPERTS, lines), 1) // (2 * QTR) == iota((EXPERTS, lines), 0)).astype(BF16)
    high = weight.astype(BF16)
    low = (weight - high.astype(F32)).astype(BF16)
    stack = jnp.concatenate([named.astype(BF16), earlier.astype(BF16), high, low], axis=0)
    wide = dot(stack, spread)
    named, earlier, high, low = (wide[i * TOK : (i + 1) * TOK] for i in range(4))
    col = iota((TOK, lines), 1)
    slot = (col % (2 * QTR)) // QTR
    chosen = jnp.logical_and(named > 0.5, jnp.abs(earlier - slot.astype(F32)) < 0.5)
    sel = []
    for q in range(QTR):
        here = jnp.logical_and(chosen, col % QTR == q)
        sel.append(jnp.where(here, 1.0, 0.0))
        mix_ref[q * TOK : (q + 1) * TOK, :] = jnp.where(here, high, 0.0).astype(BF16)
        mix_ref[(QTR + q) * TOK : (QTR + q + 1) * TOK, :] = jnp.where(here, low, 0.0).astype(BF16)
    send_ref[...] = jnp.concatenate(sel, axis=0).T.astype(BF16)


def route(ids, w):
    lines = EXPERTS * 2 * QTR
    return pl.pallas_call(
        route_body,
        out_shape=(
            jax.ShapeDtypeStruct((lines, QTR * TOK), BF16),
            jax.ShapeDtypeStruct((2 * QTR * TOK, lines), BF16),
        ),
        compiler_params=params(),
        name="route",
    )(ids, w)


def dispatch_body(parts_ref, hid_ref, gain_ref, send_ref, res_ref, out_ref):
    total = parts_ref[0].astype(F32)
    for i in range(1, parts_ref.shape[0]):
        total = total + parts_ref[i].astype(F32)
    residual = hid_ref[...].astype(F32) + total
    res_ref[...] = residual
    mean = jnp.mean(residual * residual, axis=-1, keepdims=True)
    norm = (residual * lax.rsqrt(mean + 1e-06) * gain_ref[...].astype(F32)).astype(BF16)
    tall = jnp.concatenate([norm[:, q * WIDE : (q + 1) * WIDE] for q in range(QTR)], axis=0)
    out_ref[...] = dot(send_ref[...], tall).astype(BF16)


def dispatch(parts, hid, gain, send):
    return pl.pallas_call(
        dispatch_body,
        out_shape=(
            jax.ShapeDtypeStruct((TOK, D), F32),
            jax.ShapeDtypeStruct((send.shape[0], WIDE), BF16),
        ),
        compiler_params=params(),
        name="dispatch",
    )(parts, hid, gain, send)


def expert_body(x_hbm, wg_hbm, wu_hbm, wd_hbm, out_hbm, x, wg, wu, wd, mid, res, back, sems, xsem, osem):
    lines = x.shape[0]
    rows = lines // QTR
    group = rows // 4
    load_x = pltpu.make_async_copy(x_hbm, x, xsem)
    load_x.start()
    loads_g, loads_u, loads_d = [], [], []
    for q in range(QTR):
        span = pl.ds(q * WIDE, WIDE)
        loads_g.append(pltpu.make_async_copy(wg_hbm.at[0, span, :], wg.at[span, :], sems.at[0, q]))
        loads_u.append(pltpu.make_async_copy(wu_hbm.at[0, span, :], wu.at[span, :], sems.at[1, q]))
        loads_d.append(pltpu.make_async_copy(wd_hbm.at[0, :, span], wd.at[:, span], sems.at[2, q]))
    for q in range(QTR):
        loads_g[q].start()
        loads_u[q].start()
    for q in range(QTR):
        loads_d[q].start()
    n = lines // 4
    out_row, in_row = iota((n, n), 0), iota((n, n), 1)
    perm = (in_row == (out_row % group) * QTR + out_row // group).astype(BF16)
    unperm = (out_row == (in_row % group) * QTR + in_row // group).astype(BF16)
    load_x.wait()
    sorted_rows = [dot(perm, x[i * n : (i + 1) * n, :]).astype(BF16) for i in range(4)]
    gate = jnp.zeros((rows, FF), F32)
    up = jnp.zeros((rows, FF), F32)
    for q in range(QTR):
        xq = jnp.concatenate([r[q * group : (q + 1) * group] for r in sorted_rows], axis=0)
        span = pl.ds(q * WIDE, WIDE)
        loads_g[q].wait()
        gate = gate + dot(xq, wg[span, :])
        loads_u[q].wait()
        up = up + dot(xq, wu[span, :])
    mid[...] = (gate / (1.0 + jnp.exp(-gate)) * up).astype(BF16)
    for q in range(QTR):
        loads_d[q].wait()
        res[q] = dot(mid[...], wd[:, q * WIDE : (q + 1) * WIDE]).astype(BF16)
    stores = []
    for i in range(4):
        part = res[:, i * group : (i + 1) * group, :].reshape(n, WIDE)
        back[i * n : (i + 1) * n, :] = dot(unperm, part).astype(BF16)
        stores.append(
            pltpu.make_async_copy(back.at[i * n : (i + 1) * n, :], out_hbm.at[i * n : (i + 1) * n, :], osem.at[i])
        )
        stores[-1].start()
    for st in stores:
        st.wait()


def expert(x, wg, wu, wd):
    lines = x.shape[0]
    hbm = pl.BlockSpec(memory_space=pl.ANY)
    return pl.pallas_call(
        expert_body,
        in_specs=[hbm] * 4,
        out_specs=hbm,
        out_shape=jax.ShapeDtypeStruct(x.shape, BF16),
        scratch_shapes=[
            pltpu.VMEM(x.shape, BF16),
            pltpu.VMEM((D, FF), BF16),
            pltpu.VMEM((D, FF), BF16),
            pltpu.VMEM((FF, D), BF16),
            pltpu.VMEM((lines // QTR, FF), BF16),
            pltpu.VMEM((QTR, lines // QTR, WIDE), BF16),
            pltpu.VMEM(x.shape, BF16),
            pltpu.SemaphoreType.DMA((3, QTR)),
            pltpu.SemaphoreType.DMA,
            pltpu.SemaphoreType.DMA((4,)),
        ],
        compiler_params=params(),
        cost_estimate=pl.CostEstimate(
            flops=6 * (lines // QTR) * D * FF, bytes_accessed=26 * 1024 * 1024, transcendentals=lines * FF // QTR
        ),
        name="expert",
    )(x, wg, wu, wd)


def combine_body(mix_ref, back_ref, res_ref, out_ref):
    both = dot(mix_ref[...], back_ref[...])
    n = QTR * TOK
    y = both[:n] + both[n:]
    for q in range(QTR):
        span = slice(q * WIDE, (q + 1) * WIDE)
        out_ref[:, span] = (res_ref[:, span] + y[q * TOK : (q + 1) * TOK]).astype(BF16)


def combine(mix, back, res):
    return pl.pallas_call(
        combine_body,
        out_shape=jax.ShapeDtypeStruct((TOK, D), BF16),
        compiler_params=params(),
        name="combine",
    )(mix, back, res)


def on_device(
    hidden,
    query,
    prefill_cache,
    suffix_cache,
    suffix_len,
    new_latent,
    w_uv,
    w_out,
    ffn_gain,
    expert_ids,
    route_weights,
    w_gate,
    w_up,
    w_down,
):
    samples = query.shape[1]
    n_smp = lax.axis_size("smp")
    chips = n_smp // 2
    prompts, span, width = prefill_cache.shape[1:]
    core = lax.axis_index("smp") % 2
    pair = [(i, i ^ 1) for i in range(n_smp)]
    same_core = [[2 * k + c for k in range(chips)] for c in range(2)]

    shared = n_smp // prompts // 2
    slab = prefill_cache[0].reshape(prompts, 1, 2, span // 2, width)
    outgoing = jnp.broadcast_to(slab, (prompts, shared, 2, span // 2, width)).reshape(n_smp, span // 2, width)
    half_a = lax.all_to_all(outgoing, "smp", 0, 0, tiled=True).reshape(-1, width)
    half_b = lax.ppermute(half_a, "smp", pair)

    uv_b = lax.ppermute(w_uv, "smp", pair)
    out_b = lax.ppermute(w_out, "smp", pair)
    send, mix = route(expert_ids.reshape(TOK, TOP), route_weights.reshape(TOK, TOP))

    context = attend(
        suffix_len, query.reshape(samples, STEPS * HEADS, width), half_a, half_b, suffix_cache[0], new_latent[0]
    )
    by_chip = context.reshape(chips, HEADS // chips, TOK, LAT)
    by_heads = lax.all_to_all(by_chip, "smp", 0, 0, tiled=True, axis_index_groups=same_core)
    shares = project(core.reshape(1), by_heads, w_uv, uv_b, w_out, out_b)
    parts = lax.all_to_all(shares, "smp", 0, 0, tiled=True, axis_index_groups=same_core)
    residual, rows = dispatch(parts, hidden.reshape(TOK, D), ffn_gain.reshape(1, D), send)

    rows = rows.reshape(EXPERTS, 2 * QTR, WIDE)
    arrived = lax.all_to_all(rows, ("grp", "smp"), 0, 0, tiled=True)
    answered = expert(arrived.reshape(-1, WIDE), w_gate, w_up, w_down)
    answered = answered.reshape(EXPERTS, 2 * QTR, WIDE)
    returned = lax.all_to_all(answered, ("grp", "smp"), 0, 0, tiled=True)
    layer_out = combine(mix, returned.reshape(-1, WIDE), residual)
    return layer_out.reshape(hidden.shape)


def solution(mesh):
    placed = (
        P("grp", "smp", None, None),
        P("grp", "smp", None, None, None),
        P("grp", None, "smp", None),
        P("grp", "smp", None, None),
        P("grp", "smp"),
        P("grp", "smp", None, None),
        P("smp", None, None),
        P("smp", None, None),
        P(),
        P("grp", "smp", None, None),
        P("grp", "smp", None, None),
        P(("grp", "smp"), None, None),
        P(("grp", "smp"), None, None),
        P(("grp", "smp"), None, None),
    )
    return jax.shard_map(
        on_device,
        mesh=mesh,
        in_specs=placed,
        out_specs=P("grp", "smp", None, None),
        check_vma=False,
    )
```

time: 338 us -> 204 us (0.60)
  waiting for transfers between devices: 186 us -> 36.1 us
  Pallas kernels: 0 us -> 44.8 us
  blocking collectives: 58.9 us -> 101 us
  matrix products: 32.8 us -> 0 us
  local copies, waits for them, and re-layouts: 36.2 us -> 13.1 us
  between operations: 13.7 us -> 0.07 us
  other arithmetic: 5.46 us -> 0 us
  starting transfers between devices: 4.64 us -> 8.42 us
    all_gather x1 -> x0, waiting for transfers between devices: 81.4 us -> none  [on_device(): gathered = lax.all_gather(slab, 'smp', axis=1, tiled=True)]
    reduce_scatter x1 -> x0, waiting for transfers between devices: 76 us -> none  [on_device(): lax.psum_scatter(jnp.einsum('rhv,hvd->rd', head_value, w_out, preferred_e...]
    pallas_call x0 -> x6, Pallas kernels: none -> 44.8 us  [the longest x1 17.6 us: expert(): pl.pallas_call(expert_body, in_specs=[hbm] * 4, out_specs=hbm, out_shape=...]
    all_to_all x2 -> x3, blocking collectives: 58.9 us -> 101 us  [the longest x1 37.9 us: on_device(): arrived = lax.all_to_all(rows, ('grp', 'smp'), 0, 0, tiled=True)]
    dot_general x9 -> x0, matrix products: 32.8 us -> none  [the longest x1 10.8 us: on_device(): jnp.dot(middle, w_down[0], preferred_element_type=jnp.float32)]
    reshape x5 -> x3, local copies, waits for them, and re-layouts: 15.2 us -> 2.71 us  [the longest x1 1.42 us: on_device(): lax.all_to_all(outgoing, 'smp', 0, 0, tiled=True).reshape(-1, width)]
    dynamic_slice x2 -> x0, local copies, waits for them, and re-layouts: 7.94 us -> none  [on_device(): prefix = lax.dynamic_index_in_dim(gathered, prompt_here, 0, keepdims=False)]
    all_to_all x1 -> x2, waiting for transfers between devices: 27.8 us -> 34.9 us  [the longest x1 19.7 us: on_device(): lax.all_to_all(shares, 'smp', 0, 0, tiled=True, axis_index_groups=same_core)]
  transfers between devices with their start and end apart: 3 -> 5, of which waited for: 3 -> 3; matrix products, arithmetic and copies ran while one was open for 2% -> 3% of each run, Pallas kernels for 0% -> 7%
where the time goes in v1:
time: 204 us
  blocking collectives  101 us (50%)
  Pallas kernels  44.8 us (22%)
  waiting for transfers between devices  36.1 us (18%)
  local copies, waits for them, and re-layouts  13.1 us (6%)
  starting transfers between devices  8.42 us (4%)
    all_to_all x1, blocking collectives, on_device(): arrived = lax.all_to_all(rows, ('grp', 'smp'), 0, 0, tiled=True)  37.9 us
    all_to_all x1, blocking collectives, on_device(): returned = lax.all_to_all(answered, ('grp', 'smp'), 0, 0, tiled=True)  33.4 us
    all_to_all x1, blocking collectives, on_device(): lax.all_to_all(outgoing, 'smp', 0, 0, tiled=True).reshape(-1, width)  29.6 us
    all_to_all x1, waiting for transfers between devices, on_device(): lax.all_to_all(shares, 'smp', 0, 0, tiled=True, axis_index_groups=same_core)  19.7 us
    pallas_call x1, Pallas kernels, expert(): pl.pallas_call(expert_body, in_specs=[hbm] * 4, out_specs=hbm, out_shape=...  17.6 us
    all_to_all x1, waiting for transfers between devices, on_device(): lax.all_to_all(by_chip, 'smp', 0, 0, tiled=True, axis_index_groups=same_c...  15.2 us
    pallas_call x1, Pallas kernels, attend(): pl.pallas_call(attend_body, grid=(samples,), in_specs=[pl.BlockSpec(memor...  13 us
    pallas_call x1, Pallas kernels, project(): pl.pallas_call(project_body, grid=(QTR,), in_specs=[pl.BlockSpec(memory_s...  5.75 us
  transfers between devices with their start and end apart: 5, of which 3 were waited for; matrix products, arithmetic and copies ran while one was open for 3% of the time, Pallas kernels for 7%

profile of v1, /device:TPU:1, one launch (start us, length us, event | category | flops | bytes accessed | tf_op | source)
XLA Modules:
  0.0 203.5 jit_solution(6005831881336733134)
XLA Ops:
  0.0 1.3 broadcast_in_dim.8
  1.3 29.6 %all_to_all.25 = bf16[32,32,576]{2,1,0:T(8,128)(2,1)S(1)} all-to-all(bf16[32,32,576]{2,1,0:T(8,128)(2,1)S(1)} %bitcast.19), channel_id=1, replica_groups=mesh['grp'=4,'smp'=32] {'smp'}, dimensions={0} | all-to-all | bytes 2359296 | tf_op jit(solution)/shard_map/all_to_all | solution.py:332
  30.9 0.0 copy-start.1
  30.9 0.0 copy-start.3
  30.9 1.4 copy.16
  32.3 0.2 collective-permute-start
  32.5 0.8 copy-done.3
  33.3 0.2 collective-permute-start.2
  33.5 2.2 %copy.17 = bf16[1,4,128,576]{3,2,1,0:T(8,128)(2,1)} copy(bf16[1,4,128,576]{2,3,1,0:T(8,128)(2,1)} %param.17) | data formatting | bytes 1179648 | tf_op args[3]
  35.6 0.0 copy-done.1
  35.6 0.0 collective-permute-done
  35.6 2.4 %copy.18.kb_ref = bf16[1024,576]{1,0:T(8,128)(2,1)} copy(bf16[1024,576]{0,1:T(8,128)(2,1)} %collective-permute-done) | data formatting | bytes 2359296 | tf_op jit(solution)/shard_map/ppermute | solution.py:333
  38.0 13.0 %attend.1 = bf16[64,16,512]{2,1,0:T(8,128)(2,1)} custom-call(s32[1,4]{1,0:T(1,128)} %len_ref.1, bf16[4,256,576]{2,1,0:T(8,128)(2,1)} %bitcast.26, bf16[1024,576]{1,0:T(8,128)(2,1)} %bitcast.18, bf16[1024,576]{1,0:T(8,128)(2,1)} %copy.18.kb_ref, bf16[4,128,576]{2,1,0:T(8,128)(2,1)} %bitcast.22, bf16[4,4,576]{2,1,0:T(4,128)(2,1)} %bitcast.27), custom_call_target="tpu_custom_call" | custom-call | flops 4848615424 | bytes 8388608 | tf_op jit(solution)/shard_map/attend/pallas_call | solution.py:77
  51.1 0.0 copy-start.4
  51.1 3.8 %all-to-all-start.1 = ((bf16[16,4,16,512]{3,2,1,0:T(8,128)(2,1)}), bf16[16,4,16,512]{3,2,1,0:T(8,128)(2,1)S(1)}, u32[]{:S(2)}, u32[]{:S(2)}) async-start(bf16[16,4,16,512]{3,2,1,0:T(8,128)(2,1)} %bitcast.21), calls=%async_computation.1 | async-start | bytes 2097152 | tf_op jit(solution)/shard_map/all_to_all | solution.py:343
  54.9 0.0 copy-done.4
  54.9 0.4 collective-permute-start.1
  55.3 1.2 collective-permute-done.1.uvb_ref
  56.5 0.0 copy-start.5
  56.5 0.0 collective-permute-done.2.ob_ref
  56.5 15.2 %all-to-all-done.1.x_ref = bf16[16,4,16,512]{3,2,1,0:T(8,128)(2,1)S(1)} async-done(((bf16[16,4,16,512]{3,2,1,0:T(8,128)(2,1)}), bf16[16,4,16,512]{3,2,1,0:T(8,128)(2,1)S(1)}, u32[]{:S(2)}, u32[]{:S(2)}) %all-to-all-start.1) | async-done | bytes 1048608 | tf_op jit(solution)/shard_map/all_to_all | solution.py:343
  71.7 0.0 copy-start.2
  71.7 0.0 copy-done.5
  71.7 1.0 copy-done.2
  72.7 5.8 %project.1 = bf16[16,16,3584]{2,1,0:T(8,128)(2,1)} custom-call(s32[1]{0:T(128)} %bitcast.2.core_ref, bf16[16,4,16,512]{3,2,1,0:T(8,128)(2,1)} %copy-done.2, bf16[2,512,128]{2,1,0:T(8,128)(2,1)} %uva_ref.1, bf16[2,512,128]{2,1,0:T(8,128)(2,1)} %copy-done.5, bf16[2,128,3584]{2,1,0:T(8,128)(2,1)} %oa_ref.1, bf16[2,128,3584]{2,1,0:T(8,128)(2,1)} %collective-permute-done.2.ob_ref), custom_call_target="tpu_custom_call" | custom-call | flops 1100000000 | bytes 7340032 | tf_op jit(solution)/shard_map/project/pallas_call | solution.py:123
  78.4 0.0 copy-start.6
  78.4 0.0 copy-start.7
  78.4 3.9 %all-to-all-start.2 = ((bf16[16,16,3584]{2,1,0:T(8,128)(2,1)}), bf16[16,16,3584]{2,1,0:T(8,128)(2,1)S(1)}, u32[]{:S(2)}, u32[]{:S(2)}) async-start(bf16[16,16,3584]{2,1,0:T(8,128)(2,1)} %project.1), calls=%async_computation.2 | async-start | bytes 3670016 | tf_op jit(solution)/shard_map/all_to_all | solution.py:345
  82.3 0.0 copy-done.6
  82.3 0.7 reshape.50.hid_ref
  83.0 0.0 copy-done.7
  83.0 0.6 reshape.51.gain_ref
  83.6 1.9 route.1
  85.5 19.7 %all-to-all-done.2.parts_ref = bf16[16,16,3584]{2,1,0:T(8,128)(2,1)S(1)} async-done(((bf16[16,16,3584]{2,1,0:T(8,128)(2,1)}), bf16[16,16,3584]{2,1,0:T(8,128)(2,1)S(1)}, u32[]{:S(2)}, u32[]{:S(2)}) %all-to-all-start.2) | async-done | bytes 1835040 | tf_op jit(solution)/shard_map/all_to_all | solution.py:345
  105.2 0.0 copy-start
  105.3 1.2 copy-done
  106.5 3.9 %dispatch.1 = (f32[16,3584]{1,0:T(8,128)}, bf16[1024,896]{1,0:T(8,128)(2,1)}) custom-call(bf16[16,16,3584]{2,1,0:T(8,128)(2,1)} %copy-done, bf16[16,3584]{1,0:T(8,128)(2,1)} %reshape.50.hid_ref, bf16[1,3584]{1,0:T(2,128)(2,1)} %reshape.51.gain_ref, bf16[1024,64]{1,0:T(8,128)(2,1)} %get-tuple-element.10.send_ref), custom_call_target="tpu_custom_call" | custom-call | tf_op jit(solution)/shard_map/dispatch/pallas_call | solution.py:200
  110.4 37.9 %all_to_all.26 = bf16[128,8,896]{2,1,0:T(8,128)(2,1)} all-to-all(bf16[128,8,896]{2,1,0:T(8,128)(2,1)} %bitcast.20), channel_id=1, replica_groups=mesh['grp'=4,'smp'=32] {'grp','smp'}, dimensions={0} | all-to-all | bytes 3670016 | tf_op jit(solution)/shard_map/all_to_all | solution.py:349
  148.3 17.6 %expert.1 = bf16[1024,896]{1,0:T(8,128)(2,1)} custom-call(bf16[1024,896]{1,0:T(8,128)(2,1)} %bitcast.14, bf16[1,3584,1024]{2,1,0:T(8,128)(2,1)} %wg_hbm.1, bf16[1,3584,1024]{2,1,0:T(8,128)(2,1)} %wu_hbm.1, bf16[1,1024,3584]{2,1,0:T(8,128)(2,1)} %wd_hbm.1), custom_call_target="tpu_custom_call" | custom-call | flops 5637144576 | bytes 27262976 | tf_op jit(solution)/shard_map/expert/pallas_call | solution.py:262
  165.9 33.4 %all_to_all.27 = bf16[128,8,896]{2,1,0:T(8,128)(2,1)} all-to-all(bf16[128,8,896]{2,1,0:T(8,128)(2,1)} %bitcast.15), channel_id=1, replica_groups=mesh['grp'=4,'smp'=32] {'grp','smp'}, dimensions={0} | all-to-all | bytes 3670016 | tf_op jit(solution)/shard_map/all_to_all | solution.py:352
  199.3 2.7 %combine.1 = bf16[16,3584]{1,0:T(8,128)(2,1)} custom-call(bf16[128,1024]{1,0:T(8,128)(2,1)} %get-tuple-element.9.mix_ref, bf16[1024,896]{1,0:T(8,128)(2,1)} %bitcast.16, f32[16,3584]{1,0:T(8,128)} %get-tuple-element.12.res_ref), custom_call_target="tpu_custom_call" | custom-call | tf_op jit(solution)/shard_map/combine/pallas_call | solution.py:297
  202.0 1.6 reshape.56
Async XLA Ops:
  30.9 4.8 %copy-start.1 = (bf16[32,32,576]{2,1,0:T(8,128)(2,1)}, bf16[32,32,576]{2,1,0:T(8,128)(2,1)S(1)}, u32[]{:S(2)}) copy-start(bf16[32,32,576]{2,1,0:T(8,128)(2,1)S(1)} %all_to_all.25) | copy-start | bytes 3538948
  30.9 2.4 %copy-start.3 = (bf16[2,128,3584]{2,1,0:T(8,128)(2,1)S(1)}, bf16[2,128,3584]{2,1,0:T(8,128)(2,1)}, u32[]{:S(2)}) copy-start(bf16[2,128,3584]{2,1,0:T(8,128)(2,1)} %oa_ref.1) | copy-start | bytes 5505028
  32.3 3.3 %collective-permute-start = (bf16[1024,576]{0,1:T(8,128)(2,1)}, bf16[1024,576]{0,1:T(8,128)(2,1)}, u32[]{:S(2)}, u32[]{:S(2)}) collective-permute-start(bf16[1024,576]{0,1:T(8,128)(2,1)} %copy.16), channel_id=1, source_target_pairs={{0,1},{1,0},{2,3},{3,2},{4,5},{5,4},{6,7},{7,6},{8,9},{9,8},{10,11... | collective-permute-start | bytes 3538952 | tf_op jit(solution)/shard_map/ppermute | solution.py:333
  33.3 23.2 %collective-permute-start.2 = (bf16[2,128,3584]{2,1,0:T(8,128)(2,1)S(1)}, bf16[2,128,3584]{2,1,0:T(8,128)(2,1)}, u32[]{:S(2)}, u32[]{:S(2)}) collective-permute-start(bf16[2,128,3584]{2,1,0:T(8,128)(2,1)S(1)} %copy-done.3), channel_id=1, source_target_pairs={{0,1},{1,0},{2,3},{3,2},{4,5},{5,4},{6,7},{7,6},{8,9},{9,8},{10,11... | collective-permute-start | bytes 5505032 | tf_op jit(solution)/shard_map/ppermute | solution.py:336
  51.1 3.8 %copy-start.4 = (bf16[2,512,128]{2,1,0:T(8,128)(2,1)S(1)}, bf16[2,512,128]{2,1,0:T(8,128)(2,1)}, u32[]{:S(2)}) copy-start(bf16[2,512,128]{2,1,0:T(8,128)(2,1)} %uva_ref.1) | copy-start | bytes 786436
  51.1 20.6 %all-to-all-start.1 = ((bf16[16,4,16,512]{3,2,1,0:T(8,128)(2,1)}), bf16[16,4,16,512]{3,2,1,0:T(8,128)(2,1)S(1)}, u32[]{:S(2)}, u32[]{:S(2)}) async-start(bf16[16,4,16,512]{3,2,1,0:T(8,128)(2,1)} %bitcast.21), calls=%async_computation.1 | async-start | bytes 2097152 | tf_op jit(solution)/shard_map/all_to_all | solution.py:343
  54.9 1.6 collective-permute-start.1
  56.5 15.2 %copy-start.5 = (bf16[2,512,128]{2,1,0:T(8,128)(2,1)}, bf16[2,512,128]{2,1,0:T(8,128)(2,1)S(1)}, u32[]{:S(2)}) copy-start(bf16[2,512,128]{2,1,0:T(8,128)(2,1)S(1)} %collective-permute-done.1.uvb_ref) | copy-start | bytes 786436
  71.7 1.0 copy-start.2
  78.4 3.9 %copy-start.6 = (bf16[1,4,4,3584]{3,2,1,0:T(4,128)(2,1)S(1)}, bf16[1,4,4,3584]{3,2,1,0:T(4,128)(2,1)}, u32[]{:S(2)}) copy-start(bf16[1,4,4,3584]{3,2,1,0:T(4,128)(2,1)} %param.14) | copy-start | bytes 344068
  78.4 4.6 %copy-start.7 = (bf16[3584]{0:T(1024)(128)(2,1)S(1)}, bf16[3584]{0:T(1024)(128)(2,1)}, u32[]{:S(2)}) copy-start(bf16[3584]{0:T(1024)(128)(2,1)} %param.22) | copy-start | bytes 21508
  78.4 26.8 %all-to-all-start.2 = ((bf16[16,16,3584]{2,1,0:T(8,128)(2,1)}), bf16[16,16,3584]{2,1,0:T(8,128)(2,1)S(1)}, u32[]{:S(2)}, u32[]{:S(2)}) async-start(bf16[16,16,3584]{2,1,0:T(8,128)(2,1)} %project.1), calls=%async_computation.2 | async-start | bytes 3670016 | tf_op jit(solution)/shard_map/all_to_all | solution.py:345
  105.2 1.2 copy-start
